TPU v7x, 32 devices: a whole 2x2x4 slice. The times are simulated.
32 devices in a mesh: dp: 4 (over y, x), blk: 8 (over z, core).
Axes of the slice: x: 2, y: 2, z: 4, core: 2. Of those that a mesh axis runs over, the one named last changes fastest.
Arguments:
- inputs: bfloat16 [4, 2048, 1024], P('dp', 'blk'), may hold values from -6 to 6
- upstream: bfloat16 [4, 2048, 1024], P('dp', 'blk'), may hold values from -6 to 6
- gain: float32 [1024], replicated, may hold values from 0.5 to 1.5
- w_query: bfloat16 [1024, 1024], replicated
- w_key: bfloat16 [1024, 256], replicated
- w_value: bfloat16 [1024, 256], replicated, may hold values from -0.1875 to 0.1875
- w_out: bfloat16 [1024, 1024], replicated, may hold values from -0.1875 to 0.1875
- prefix_len: int32 [4], P('dp'), may hold values from 256 to 1984
- bound: int32 [4], P('dp'), may hold values from 0 to 15
Outputs:
- d_inputs: bfloat16 [4, 2048, 1024], P('dp', 'blk')
- d_query: float32 [1024, 1024], P('blk')
- d_key: float32 [1024, 256], P('blk')
- d_value: float32 [1024, 256], P('blk')
- d_out: float32 [1024, 1024], P('blk')
- d_gain: float32 [1024], P('blk')
All inputs are finite; a program needn't handle non-finite values.
Results may differ from a plain program's by a relative error of at most 0.02.
The roundings to bfloat16 on the way count: a program that leaves them out, or rounds other values in their place, can miss the bound.
Values may be sent and summed in bfloat16 or wider, within the bound.
A program may use at most 128 MiB of HBM per device.

v0:
```python
import jax
import jax.numpy as jnp
from jax import lax
from jax.sharding import PartitionSpec as P

HS = 256
ACT = 64
BLOCK = 128


EPS = 1e-06
NEG = -1e30


def contract_last(left, right):
    return lax.dot_general(
        left, right, (((1,), (1,)), ((), ())), preferred_element_type=jnp.float32
    )


def contract_first(left, right):
    return lax.dot_general(
        left, right, (((0,), (0,)), ((), ())), preferred_element_type=jnp.float32
    )


def per_device(inputs, upstream, gain, w_query, w_key, w_value, w_out, prefix_len, bound):
    tok = inputs.shape[1]
    cycle_size = lax.axis_size("blk")
    seq = tok * cycle_size
    scaling = HS ** (-0.5)
    heads = w_query.shape[1] // HS
    xf = inputs[0].astype(jnp.float32)
    grad_out = upstream[0]
    inv = lax.rsqrt(jnp.mean(xf * xf, axis=-1, keepdims=True) + EPS)
    normed = xf * inv
    hidden = (normed * gain).astype(jnp.bfloat16)
    query = jnp.dot(hidden, w_query, preferred_element_type=jnp.float32).astype(jnp.bfloat16)
    keys = jnp.dot(hidden, w_key, preferred_element_type=jnp.float32).astype(jnp.bfloat16)
    values = jnp.dot(hidden, w_value, preferred_element_type=jnp.float32).astype(jnp.bfloat16)
    d_attn = contract_last(grad_out, w_out).astype(jnp.bfloat16)
    all_keys, all_values = (
        lax.all_gather(keys, "blk", axis=0, tiled=True),
        lax.all_gather(values, "blk", axis=0, tiled=True),
    )
    q_three = query.reshape(tok, heads, HS)
    da_three = d_attn.reshape(tok, heads, HS)
    my_index = lax.axis_index("blk")
    q_pos = my_index * tok + jnp.arange(tok, dtype=jnp.int32)
    plen = prefix_len[0]
    edge = bound[0] * BLOCK
    width = min(512, seq)
    steps_count = seq // width

    def scores_of(key_rows, key_start):
        scores = (
            jnp.einsum("thd,kd->htk", q_three, key_rows, preferred_element_type=jnp.float32)
            * scaling
        )
        k_pos = key_start + jnp.arange(key_rows.shape[0], dtype=jnp.int32)
        key_ok = (k_pos < plen) | (k_pos >= seq - ACT)
        visible = key_ok[None, :] & ((k_pos[None, :] < edge) | (k_pos[None, :] <= q_pos[:, None]))
        return jnp.where(visible[None], scores, NEG)

    def take(array, index):
        return lax.dynamic_slice_in_dim(array, index * width, width, 0)

    def stat_step(index, carry):
        top, total = carry
        scores = scores_of(take(all_keys, index), index * width)
        new_top = jnp.maximum(top, jnp.max(scores, axis=-1))
        total = total * jnp.exp(top - new_top) + jnp.sum(
            jnp.exp(scores - new_top[..., None]), axis=-1
        )
        return (new_top, total)

    start_top = jnp.full((heads, tok), NEG, jnp.float32)
    top, total = lax.fori_loop(
        0, steps_count, stat_step, (start_top, jnp.zeros((heads, tok), jnp.float32))
    )

    def probs_of(scores):
        return jnp.exp(scores - top[..., None]) / total[..., None]

    def attn_step(index, acc):
        probs_b = probs_of(scores_of(take(all_keys, index), index * width)).astype(jnp.bfloat16)
        return acc + jnp.einsum(
            "htk,kd->thd", probs_b, take(all_values, index), preferred_element_type=jnp.float32
        )

    attn_acc = lax.fori_loop(0, steps_count, attn_step, jnp.zeros((tok, heads, HS), jnp.float32))
    attn_three = attn_acc.astype(jnp.bfloat16)
    attn = attn_three.reshape(tok, heads * HS)
    delta = jnp.sum(da_three.astype(jnp.float32) * attn_three.astype(jnp.float32), axis=-1).T

    def grads_of(key_rows, value_rows, key_start):
        probs = probs_of(scores_of(key_rows, key_start))
        probs_b = probs.astype(jnp.bfloat16)
        dprobs = jnp.einsum("thd,kd->htk", da_three, value_rows, preferred_element_type=jnp.float32)
        dscores = (probs * (dprobs - delta[..., None])).astype(jnp.bfloat16)
        return (probs_b, dscores)

    def query_step(index, dq_acc):
        key_rows = take(all_keys, index)
        probs_b, dscores = grads_of(key_rows, take(all_values, index), index * width)
        return dq_acc + jnp.einsum(
            "htk,kd->thd", dscores, key_rows, preferred_element_type=jnp.float32
        )

    zero_dq = jnp.zeros((tok, heads, HS), jnp.float32)
    dq_acc = lax.fori_loop(0, steps_count, query_step, zero_dq)
    key_rows = all_keys
    value_rows = all_values
    probs_b, dscores = grads_of(key_rows, value_rows, jnp.int32(0))
    d_k = jnp.einsum("htk,thd->kd", dscores, q_three, preferred_element_type=jnp.float32) * scaling
    d_v = jnp.einsum("htk,thd->kd", probs_b, da_three, preferred_element_type=jnp.float32)
    mine = lax.psum_scatter(
        jnp.concatenate([d_k, d_v], axis=1), "blk", scatter_dimension=0, tiled=True
    )
    d_query_rows = (dq_acc * scaling).astype(jnp.bfloat16).reshape(tok, heads * HS)
    d_key_rows = mine[:, :HS].astype(jnp.bfloat16)
    d_value_rows = mine[:, HS:].astype(jnp.bfloat16)
    dhidden = (
        contract_last(d_query_rows, w_query)
        + contract_last(d_key_rows, w_key)
        + contract_last(d_value_rows, w_value)
    )
    g_query = contract_first(hidden, d_query_rows)
    g_key = contract_first(hidden, d_key_rows)
    g_value = contract_first(hidden, d_value_rows)
    g_out = contract_first(attn, grad_out)
    g_gain = jnp.sum(dhidden * normed, axis=0)
    scaled = dhidden * gain
    d_in = grad_out.astype(jnp.float32) + inv * (
        scaled - normed * jnp.mean(scaled * normed, axis=-1, keepdims=True)
    )
    shares = (
        lax.psum_scatter(
            g_query.astype(jnp.bfloat16), "blk", scatter_dimension=0, tiled=True
        ).astype(jnp.float32),
        lax.psum_scatter(g_key.astype(jnp.bfloat16), "blk", scatter_dimension=0, tiled=True).astype(
            jnp.float32
        ),
        lax.psum_scatter(
            g_value.astype(jnp.bfloat16), "blk", scatter_dimension=0, tiled=True
        ).astype(jnp.float32),
        lax.psum_scatter(g_out.astype(jnp.bfloat16), "blk", scatter_dimension=0, tiled=True).astype(
            jnp.float32
        ),
        lax.psum_scatter(
            g_gain.astype(jnp.bfloat16), "blk", scatter_dimension=0, tiled=True
        ).astype(jnp.float32),
    )
    shares = (
        lax.psum(shares[0].astype(jnp.bfloat16), "dp").astype(jnp.float32),
        lax.psum(shares[1].astype(jnp.bfloat16), "dp").astype(jnp.float32),
        lax.psum(shares[2].astype(jnp.bfloat16), "dp").astype(jnp.float32),
        lax.psum(shares[3].astype(jnp.bfloat16), "dp").astype(jnp.float32),
        lax.psum(shares[4].astype(jnp.bfloat16), "dp").astype(jnp.float32),
    )
    return (d_in.astype(jnp.bfloat16)[None], shares[0], shares[1], shares[2], shares[3], shares[4])


def solution(mesh):
    placed = (P("dp", "blk", None), P("dp", "blk", None), P(), P(), P(), P(), P(), P("dp"), P("dp"))
    return jax.shard_map(
        per_device,
        mesh=mesh,
        in_specs=placed,
        out_specs=(
            P("dp", "blk", None),
            P("blk", None),
            P("blk", None),
            P("blk", None),
            P("blk", None),
            P("blk"),
        ),
        check_vma=False,
    )
```

profile of v0, /device:TPU:0, one launch (start us, length us, event | category | flops | bytes accessed | tf_op | source)
XLA Modules:
  0.0 352.1 jit_solution(14679281729447113167)
XLA Ops:
  8.6 2.2 convolution_convert_fusion.7
  16.4 1.9 copy.55
  18.3 3.3 convolution_convert_fusion.4
  21.6 2.2 reshape.354
  23.9 2.1 copy.34
  26.0 2.3 fusion.87
  28.3 7.6 %all-gather.3.cloned.1.call-done = bf16[2048,256]{1,0:T(8,128)(2,1)} async-done(((bf16[256,256]{1,0:T(8,128)(2,1)}), bf16[2048,256]{1,0:T(8,128)(2,1)}) %all-gather.3.cloned.1.call-update) | async-done | bytes 1048592 | tf_op jit(solution)/shard_map/all_gather | solution.py:43
  35.9 12.5 %while.44 = (s32[]{:T(128)}, f32[4,256]{1,0:T(4,128)S(1)}, f32[4,256]{1,0:T(4,128)S(1)}, s32[]{:T(128)}, s32[]{:T(128)}, /*index=5*/bf16[2048,256]{1,0:T(8,128)(...) while((s32[]{:T(128)}, f32[4,256]{1,0:T(4,128)S(1)}, ...), condition=%wide.region_4.5_spmd.clone, body=%wide.region_1.4_spmd.clone.sunk | while | flops 272507136 | bytes 5435598 | solution.py:78
  36.8 1.6 fusion.157
  40.0 1.6 fusion.157
  43.1 1.7 fusion.157
  46.3 1.6 fusion.157
  48.4 11.4 %all-gather.5.cloned.1.call-done = bf16[2048,256]{1,0:T(8,128)(2,1)} async-done(((bf16[256,256]{1,0:T(8,128)(2,1)}), bf16[2048,256]{1,0:T(8,128)(2,1)}) %all-gather.5.cloned.1.call-update) | async-done | bytes 1048592 | tf_op jit(solution)/shard_map/all_gather | solution.py:44
  59.8 17.2 %while.45 = (s32[]{:T(128)}, f32[256,4,256]{0,2,1:T(8,128)}, bf16[2048,256]{1,0:T(8,128)(2,1)}, s32[]{:T(128)}, s32[]{:T(128)}, /*index=5*/bf16[2048,256]{1,0:T(...) while((s32[]{:T(128)}, f32[256,4,256]{0,2,1:T(8,128)}, ...), condition=%wide.region_6.7_spmd.clone, body=%wide.region_5.6_spmd.clone.sunk | while | flops 540413184 | bytes 3426008 | solution.py:91
  60.7 3.2 fusion.163
  64.7 3.5 %fusion.163 = f32[256,4,256]{0,2,1:T(8,128)} fusion(f32[256,4,256]{0,2,1:T(8,128)} %get-tuple-element.1013, f32[4,256]{1,0:T(4,128)S(1)} %get-tuple-element.1034, f32[4,256]{1,0:T(4,128)S(1)} %get-tuple-element.1033, pred[256,512]{1,0:T(8,128)(4,1)S(1)} %or_and_fusion.7, bf16[256,4,256]{2,1,0:T(4,128)(2,1)S(1)} %get-tuple-element.1032, ...), kind=kOutput, calls=%fused_computation.26.clone.1 | convolution fusion | flops 540016640 | bytes 3286528 | tf_op jit(solution)/shard_map/while/body/eval_jaxpr/htk,kd->thd/dot_general | solution.py:87
  69.1 3.5 %fusion.163 = f32[256,4,256]{0,2,1:T(8,128)} fusion(f32[256,4,256]{0,2,1:T(8,128)} %get-tuple-element.1013, f32[4,256]{1,0:T(4,128)S(1)} %get-tuple-element.1034, f32[4,256]{1,0:T(4,128)S(1)} %get-tuple-element.1033, pred[256,512]{1,0:T(8,128)(4,1)S(1)} %or_and_fusion.7, bf16[256,4,256]{2,1,0:T(4,128)(2,1)S(1)} %get-tuple-element.1032, ...), kind=kOutput, calls=%fused_computation.26.clone.1 | convolution fusion | flops 540016640 | bytes 3286528 | tf_op jit(solution)/shard_map/while/body/eval_jaxpr/htk,kd->thd/dot_general | solution.py:87
  73.4 3.5 %fusion.163 = f32[256,4,256]{0,2,1:T(8,128)} fusion(f32[256,4,256]{0,2,1:T(8,128)} %get-tuple-element.1013, f32[4,256]{1,0:T(4,128)S(1)} %get-tuple-element.1034, f32[4,256]{1,0:T(4,128)S(1)} %get-tuple-element.1033, pred[256,512]{1,0:T(8,128)(4,1)S(1)} %or_and_fusion.7, bf16[256,4,256]{2,1,0:T(4,128)(2,1)S(1)} %get-tuple-element.1032, ...), kind=kOutput, calls=%fused_computation.26.clone.1 | convolution fusion | flops 540016640 | bytes 3286528 | tf_op jit(solution)/shard_map/while/body/eval_jaxpr/htk,kd->thd/dot_general | solution.py:87
  77.0 2.4 copy.26
  79.4 1.6 multiply_reduce_fusion
  81.1 3.9 %fusion.79 = f32[4,256,2048]{1,2,0:T(8,128)S(1)} fusion(f32[4,256]{1,0:T(4,128)S(1)} %get-tuple-element.1131, f32[4,256]{1,0:T(4,128)S(1)} %get-tuple-element.1118, pred[256,2048]{0,1:T(8,128)(4,1)} %fusion.87, bf16[2048,256]{1,0:T(8,128)(2,1)} %get-tuple-element.1112, bf16[32,4,8,256]{3,2,1,0:T(8,128)(2,1)} %bitcast.206), kind=kOutput, calls=%fused_computation.88 | convolution fusion | flops 1082130432 | bytes 10493952 | tf_op jit(solution)/shard_map/thd,kd->htk/dot_general | solution.py:57
  85.0 3.2 copy-done.1
  88.2 2.6 fusion.82
  90.8 7.6 %fusion.85 = f32[2048,256]{0,1:T(8,128)} fusion(f32[4,256,2048]{1,2,0:T(8,128)} %copy-done.1, bf16[256,4,256]{0,2,1:T(8,128)(2,1)} %copy.34, f32[4,256]{1,0:T(4,128)S(1)} %copy.28, bf16[2048,256]{1,0:T(8,128)(2,1)} %get-tuple-element.1139, bf16[32,4,8,256]{3,2,1,0:T(8,128)(2,1)} %bitcast.207), kind=kOutput, calls=%fused_computation.94 | convolution fusion | flops 2154299392 | bytes 12587008 | tf_op jit(solution)/shard_map/htk,thd->kd/dot_general | solution.py:115
  98.4 4.7 %pad_maximum_fusion = f32[2048,512]{0,1:T(8,128)} fusion(f32[2048,256]{0,1:T(8,128)} %fusion.82, f32[2048,256]{0,1:T(8,128)} %fusion.85), kind=kLoop, calls=%fused_computation.89 | loop fusion | flops 1048576 | bytes 8388608 | tf_op jit(solution)/shard_map/concatenate | solution.py:118
  103.3 32.2 %while.46 = (s32[]{:T(128)}, f32[256,4,256]{0,2,1:T(8,128)}, bf16[2048,256]{1,0:T(8,128)(2,1)}, s32[]{:T(128)}, s32[]{:T(128)}, /*index=5*/bf16[256,4,256]{2,1,0...) while((s32[]{:T(128)}, f32[256,4,256]{0,2,1:T(8,128)}, ...), condition=%wide.region_9.10_spmd.clone, body=%wide.region_8.9_spmd.clone.sunk | while | flops 809897216 | bytes 8410860 | solution.py:111
  104.2 2.7 fusion.169
  106.9 4.3 %fusion.171 = f32[256,4,256]{0,2,1:T(8,128)} fusion(f32[512,256,4]{0,1,2:T(8,128)} %fusion.169, f32[256,4,256]{0,2,1:T(8,128)} %get-tuple-element.1057, f32[4,256]{1,0:T(4,128)S(1)} %get-tuple-element.1082, f32[4,256]{1,0:T(4,128)S(1)} %get-tuple-element.1079, f32[4,256]{1,0:T(4,128)S(1)} %get-tuple-element.1078, ...), kind=kOutput, calls=%fused_computation.55.clone.1 | convolution fusion | flops 541065216 | bytes 5387776 | tf_op jit(solution)/shard_map/while/body/eval_jaxpr/htk,kd->thd/dot_general | solution.py:106
  112.1 2.7 fusion.169
  114.8 4.5 %fusion.171 = f32[256,4,256]{0,2,1:T(8,128)} fusion(f32[512,256,4]{0,1,2:T(8,128)} %fusion.169, f32[256,4,256]{0,2,1:T(8,128)} %get-tuple-element.1057, f32[4,256]{1,0:T(4,128)S(1)} %get-tuple-element.1082, f32[4,256]{1,0:T(4,128)S(1)} %get-tuple-element.1079, f32[4,256]{1,0:T(4,128)S(1)} %get-tuple-element.1078, ...), kind=kOutput, calls=%fused_computation.55.clone.1 | convolution fusion | flops 541065216 | bytes 5387776 | tf_op jit(solution)/shard_map/while/body/eval_jaxpr/htk,kd->thd/dot_general | solution.py:106
  120.1 2.8 fusion.169
  122.9 4.5 %fusion.171 = f32[256,4,256]{0,2,1:T(8,128)} fusion(f32[512,256,4]{0,1,2:T(8,128)} %fusion.169, f32[256,4,256]{0,2,1:T(8,128)} %get-tuple-element.1057, f32[4,256]{1,0:T(4,128)S(1)} %get-tuple-element.1082, f32[4,256]{1,0:T(4,128)S(1)} %get-tuple-element.1079, f32[4,256]{1,0:T(4,128)S(1)} %get-tuple-element.1078, ...), kind=kOutput, calls=%fused_computation.55.clone.1 | convolution fusion | flops 541065216 | bytes 5387776 | tf_op jit(solution)/shard_map/while/body/eval_jaxpr/htk,kd->thd/dot_general | solution.py:106
  128.2 2.8 fusion.169
  131.0 4.5 %fusion.171 = f32[256,4,256]{0,2,1:T(8,128)} fusion(f32[512,256,4]{0,1,2:T(8,128)} %fusion.169, f32[256,4,256]{0,2,1:T(8,128)} %get-tuple-element.1057, f32[4,256]{1,0:T(4,128)S(1)} %get-tuple-element.1082, f32[4,256]{1,0:T(4,128)S(1)} %get-tuple-element.1079, f32[4,256]{1,0:T(4,128)S(1)} %get-tuple-element.1078, ...), kind=kOutput, calls=%fused_computation.55.clone.1 | convolution fusion | flops 541065216 | bytes 5387776 | tf_op jit(solution)/shard_map/while/body/eval_jaxpr/htk,kd->thd/dot_general | solution.py:106
  137.6 2.2 convolution_convert_fusion.1
  140.0 3.2 convolution_convert_fusion
  143.2 9.6 %reduce-scatter.6.cloned.1.call-done = f32[256,512]{0,1:T(8,128)} async-done(((f32[2048,512]{0,1:T(8,128)}), f32[256,512]{0,1:T(8,128)}) %reduce-scatter.6.cloned.1.call-update) | async-done | bytes 524304 | tf_op jit(solution)/shard_map/reduce_scatter | solution.py:117
  160.2 28.7 %reduce-scatter.8.cloned.1.call-done = bf16[128,1024]{1,0:T(8,128)(2,1)} async-done(((bf16[1024,1024]{1,0:T(8,128)(2,1)}), bf16[128,1024]{1,0:T(8,128)(2,1)}) %reduce-scatter.8.cloned.1.call-update) | async-done | bytes 262160 | tf_op jit(solution)/shard_map/reduce_scatter | solution.py:138
  188.9 36.5 %reduce-scatter.14.cloned.1.call-done = bf16[128,1024]{1,0:T(8,128)(2,1)} async-done(((bf16[1024,1024]{1,0:T(8,128)(2,1)}), bf16[128,1024]{1,0:T(8,128)(2,1)}) %reduce-scatter.14.cloned.1.call-update) | async-done | bytes 262160 | tf_op jit(solution)/shard_map/reduce_scatter | solution.py:147
  225.4 32.2 %reduce-scatter.10.cloned.1.call-done = bf16[128,256]{1,0:T(8,128)(2,1)} async-done(((bf16[1024,256]{1,0:T(8,128)(2,1)}), bf16[128,256]{1,0:T(8,128)(2,1)}) %reduce-scatter.10.cloned.1.call-update) | async-done | bytes 65552 | tf_op jit(solution)/shard_map/reduce_scatter | solution.py:141
  257.6 32.1 %reduce-scatter.12.cloned.1.call-done = bf16[128,256]{1,0:T(8,128)(2,1)} async-done(((bf16[1024,256]{1,0:T(8,128)(2,1)}), bf16[128,256]{1,0:T(8,128)(2,1)}) %reduce-scatter.12.cloned.1.call-update) | async-done | bytes 65552 | tf_op jit(solution)/shard_map/reduce_scatter | solution.py:144
  289.7 2.9 fusion.100
  292.6 13.7 %all-reduce = bf16[1024]{0:T(1024)(128)(2,1)S(1)} all-reduce(bf16[1024]{0:T(1024)(128)(2,1)S(1)} %get-tuple-element.686), channel_id=7, replica_groups=mesh['dp'=4,'blk'=8] {'blk'}, use_global_device_ids=true, to_apply=%region_21.22.clone | all-reduce | flops 1024 | bytes 4096
  306.3 10.1 %psum.39 = bf16[128]{0:T(256)(128)(2,1)S(1)} all-reduce(bf16[128]{0:T(256)(128)(2,1)S(1)} %dynamic-slice.1), channel_id=1, replica_groups=mesh['dp'=4,'blk'=8] {'dp'}, use_global_device_ids=true, to_apply=%region_22.23 | all-reduce | flops 128 | bytes 512 | tf_op jit(solution)/shard_map/psum | solution.py:159
  316.9 2.4 fusion.109
  319.3 19.3 %all-reduce.4.cloned.1.call-done = (bf16[128,1024]{1,0:T(8,128)(2,1)}, bf16[128,256]{1,0:T(8,128)(2,1)}, bf16[128,256]{1,0:T(8,128)(2,1)}, bf16[128,1024]{1,0:T(8,128)(2,1)}) async-done(((bf16[128,1024]{1,0:T(8,128)(2,1)}, bf16[128,256]{1,0:T(8,128)(2,1)}, bf16[128,256]{1,0:T(8,128)(2,1)}, bf16[128,1024]{1,0:T(8,128)(2,1)}), (bf16[128,1024]{1,0:T(8,128)(2,1)}, bf16[128,256]{1,0:T(8,128)(2,1)}, ...) | async-done | bytes 655376 | tf_op jit(solution)/shard_map/psum | solution.py:155
  341.6 1.8 convert_element_type.128
  343.4 1.8 convert_element_type.134
  (128 shorter events, 30.8 us)
Async XLA Ops:
  7.2 6.3 %copy-start = (bf16[1024,1024]{1,0:T(8,128)(2,1)S(1)}, bf16[1024,1024]{1,0:T(8,128)(2,1)}, u32[]{:S(2)}) copy-start(bf16[1024,1024]{1,0:T(8,128)(2,1)} %param.18) | copy-start | bytes 6291460
  7.2 3.8 %copy-start.2 = (bf16[1,256,1024]{2,1,0:T(8,128)(2,1)S(1)}, bf16[1,256,1024]{2,1,0:T(8,128)(2,1)}, u32[]{:S(2)}) copy-start(bf16[1,256,1024]{2,1,0:T(8,128)(2,1)} %param.15) | copy-start | bytes 1572868
  7.2 3.8 %copy-start.10 = (f32[1024]{0:T(1024)S(1)}, f32[1024]{0:T(1024)}, u32[]{:S(2)}) copy-start(f32[1024]{0:T(1024)} %param.17) | copy-start | bytes 12292
  7.2 3.8 %copy-start.8 = (bf16[1024,256]{1,0:T(8,128)(2,1)S(1)}, bf16[1024,256]{1,0:T(8,128)(2,1)}, u32[]{:S(2)}) copy-start(bf16[1024,256]{1,0:T(8,128)(2,1)} %param.20) | copy-start | bytes 1572868
  7.2 28.6 %all-gather.3.cloned.1.call-start = ((), (), s32[]{:S(2)}) async-start(), calls=%async_computation.5 | async-start | bytes 1179648 | tf_op jit(solution)/shard_map/all_gather | solution.py:43
  10.9 48.9 %all-gather.5.cloned.1.call-start = ((), (), s32[]{:S(2)}) async-start(), calls=%async_computation.6 | async-start | bytes 1179648 | tf_op jit(solution)/shard_map/all_gather | solution.py:44
  12.0 140.8 %reduce-scatter.6.cloned.1.call-start = ((), (), s32[]{:S(2)}) async-start(), calls=%async_computation.7 | async-start | bytes 4718592 | tf_op jit(solution)/shard_map/reduce_scatter | solution.py:117
  81.1 7.1 %copy-start.6 = (bf16[256,4,256]{0,2,1:T(8,128)(2,1)S(1)}, bf16[256,4,256]{0,2,1:T(8,128)(2,1)}, u32[]{:S(2)}) copy-start(bf16[256,4,256]{0,2,1:T(8,128)(2,1)} %copy.34) | copy-start | bytes 1572868
  84.9 3.2 copy-start.1
  103.1 85.8 %reduce-scatter.8.cloned.1.call-start = ((), (), s32[]{:S(2)}) async-start(), calls=%async_computation.8 | async-start | bytes 2359296 | tf_op jit(solution)/shard_map/reduce_scatter | solution.py:138
  136.8 0.8 copy-start.4
  137.6 2.3 copy-start.3
  139.8 85.6 %reduce-scatter.14.cloned.1.call-start = ((), (), s32[]{:S(2)}) async-start(), calls=%async_computation.11 | async-start | bytes 2359296 | tf_op jit(solution)/shard_map/reduce_scatter | solution.py:147
  143.1 114.5 %reduce-scatter.10.cloned.1.call-start = ((), (), s32[]{:S(2)}) async-start(), calls=%async_computation.9 | async-start | bytes 589824 | tf_op jit(solution)/shard_map/reduce_scatter | solution.py:141
  153.9 2.7 copy-start.11
  153.9 3.9 %copy-start.5 = (bf16[256,4,256]{0,2,1:T(8,128)(2,1)S(1)}, bf16[256,4,256]{0,2,1:T(8,128)(2,1)}, u32[]{:S(2)}) copy-start(bf16[256,4,256]{0,2,1:T(8,128)(2,1)} %copy-done.4) | copy-start | bytes 1572868
  155.2 134.5 %reduce-scatter.12.cloned.1.call-start = ((), (), s32[]{:S(2)}) async-start(), calls=%async_computation.10 | async-start | bytes 589824 | tf_op jit(solution)/shard_map/reduce_scatter | solution.py:144
  156.5 182.1 %all-reduce.4.cloned.1.call-start = ((), (), s32[]{:S(2)}) async-start(), calls=%async_computation.12 | async-start | bytes 1310720 | tf_op jit(solution)/shard_map/psum | solution.py:155
  157.8 1.0 copy-start.9
  160.2 156.7 %copy-start.7 = (bf16[1,256,1024]{2,1,0:T(8,128)(2,1)S(1)}, bf16[1,256,1024]{2,1,0:T(8,128)(2,1)}, u32[]{:S(2)}) copy-start(bf16[1,256,1024]{2,1,0:T(8,128)(2,1)} %param.16) | copy-start | bytes 1572868
Sparse Core Ops, SparseCore 0:
  11.0 24.7 all-gather.2
  38.0 21.7 all-gather.4
  103.2 49.5 reduce-scatter.5
  155.0 33.8 reduce-scatter.7
  191.0 34.3 reduce-scatter.13
  228.1 29.4 reduce-scatter.9
  260.5 29.0 reduce-scatter.11
  292.9 45.6 all-reduce.3
where the time goes:
time: 353 us; the launch traced here: 352 us
  waiting for transfers between devices  178 us (50%)
  matrix products  84 us (24%)
  other arithmetic  34.1 us (10%)
  blocking collectives  23.8 us (7%)
  between operations  16.3 us (5%)
  local copies, waits for them, and re-layouts  15.2 us (4%)
    reduce_scatter x1, waiting for transfers between devices, per_device(): lax.psum_scatter(g_out.astype(jnp.bfloat16), 'blk', scatter_dimension=0,...  36.5 us
    reduce_scatter x1, waiting for transfers between devices, per_device(): lax.psum_scatter(g_key.astype(jnp.bfloat16), 'blk', scatter_dimension=0,...  32.2 us
    reduce_scatter x1, waiting for transfers between devices, per_device(): lax.psum_scatter(g_value.astype(jnp.bfloat16), 'blk', scatter_dimension=0...  32.1 us
    reduce_scatter x1, waiting for transfers between devices, per_device(): lax.psum_scatter(g_query.astype(jnp.bfloat16), 'blk', scatter_dimension=0...  28.7 us
    dot_general x9, matrix products, scores_of(): jnp.einsum('thd,kd->htk', q_three, key_rows, preferred_element_type=jnp.f...  21.5 us
    psum x1, waiting for transfers between devices, per_device(): lax.psum(shares[0].astype(jnp.bfloat16), 'dp').astype(jnp.float32)  19.3 us
    dot_general x4, matrix products, query_step(): jnp.einsum('htk,kd->thd', dscores, key_rows, preferred_element_type=jnp.f...  17.7 us
    dot_general x4, matrix products, attn_step(): jnp.einsum('htk,kd->thd', probs_b, take(all_values, index), preferred_ele...  13.7 us
  transfers between devices with their start and end apart: 8, of which 8 were waited for; matrix products, arithmetic and copies ran while one was open for 22% of the time, Pallas kernels for 0%

commit v1 on v0

v1 whole, which is shorter than its diff:
```python
import functools

import jax
import jax.numpy as jnp
from jax import lax
from jax.experimental import pallas as pl
from jax.experimental.pallas import tpu as pltpu
from jax.sharding import PartitionSpec as P

HS = 256
ACT = 64
BLOCK = 128
EPS = 1e-06
NEG = -1e30
CHUNK = 256
F32 = jnp.float32
BF16 = jnp.bfloat16
MESH = pl.DeviceIdType.MESH


def dot_nn(left, right):
    return lax.dot_general(left, right, (((1,), (0,)), ((), ())), preferred_element_type=F32)


def dot_nt(left, right):
    return lax.dot_general(left, right, (((1,), (1,)), ((), ())), preferred_element_type=F32)


def dot_tn(left, right):
    return lax.dot_general(left, right, (((0,), (0,)), ((), ())), preferred_element_type=F32)


class Sizes:
    def __init__(self, n_dp, n_blk, tok, width, hq):
        self.n_dp = n_dp
        self.n_blk = n_blk
        self.chips = n_blk // 2
        self.tok = tok
        self.width = width
        self.heads = hq // HS
        self.lanes = self.heads * tok
        self.rows = width // n_blk
        self.row_parts = min(n_dp, self.rows // 16)
        self.col_parts = n_dp // self.row_parts
        self.part_rows = self.rows // self.row_parts

    def item_scratch(self, cols):
        part = (self.part_rows, cols // self.col_parts)
        vm, dma = pltpu.VMEM, pltpu.SemaphoreType.DMA
        return [
            vm((self.chips, self.rows, cols), BF16),
            vm((self.chips, self.rows, cols), BF16),
            vm((self.n_dp, self.chips, *part), BF16),
            vm((self.n_dp - 1, self.chips, *part), BF16),
            vm((self.chips, *part), BF16),
            vm((self.chips - 1, *part), BF16),
            vm((self.n_dp, *part), BF16),
            dma((2,)),
            dma((2, self.n_dp)),
            dma((2, self.chips)),
            dma((2, self.n_dp)),
        ]


class Place:
    def __init__(self, sz):
        self.dp = lax.axis_index("dp")
        self.blk = lax.axis_index("blk")
        self.core = lax.rem(self.blk, 2)
        self.chip = self.blk // 2
        self.sz = sz

    def sibling(self):
        return (self.dp, 2 * self.chip + 1 - self.core)

    def chip_at(self, offset):
        return lax.rem(self.chip + offset + self.sz.chips, self.sz.chips)

    def on_chip(self, chip):
        return (self.dp, 2 * chip + self.core)

    def dp_at(self, offset):
        return lax.rem(self.dp + offset + self.sz.n_dp, self.sz.n_dp)

    def on_dp(self, dp):
        return (dp, self.blk)


def send(src, dst, sems, index, device):
    copy = pltpu.make_async_remote_copy(
        src_ref=src, dst_ref=dst, send_sem=sems.at[(0, *index)], recv_sem=sems.at[(1, *index)],
        device_id=device, device_id_type=MESH,
    )
    return copy


class Item:
    def __init__(self, place, cols, refs):
        self.at = place
        self.sz = place.sz
        self.cols = cols
        (self.pair_out, self.pair_in, self.dp_out, self.dp_in, self.z_out, self.z_in, self.final,
         self.pair_sem, self.dp_sem, self.z_sem, self.all_sem) = refs

    def product(self, lhs_ref, rhs_ref, core, first):
        sz = self.sz
        left = jnp.concatenate([lhs_ref[2 * z + core] for z in range(sz.chips)], axis=0)
        out = dot_nn(left, rhs_ref[:, first:first + CHUNK])
        return out.reshape(sz.chips, sz.rows, CHUNK)

    def pair_copy(self):
        return send(self.pair_out, self.pair_in, self.pair_sem, (), self.at.sibling())

    def dp_copy(self, e):
        peer = self.at.dp_at(e)
        return send(self.dp_out.at[peer], self.dp_in.at[e - 1], self.dp_sem, (e,), self.at.on_dp(peer))

    def z_copy(self, d):
        chip = self.at.chip_at(d)
        return send(self.z_out.at[chip], self.z_in.at[d - 1], self.z_sem, (d,), self.at.on_chip(chip))

    def all_copy(self, e):
        mine = self.final.at[self.at.dp]
        return send(mine, mine, self.all_sem, (e,), self.at.on_dp(self.at.dp_at(e)))

    def all_arrival(self, e):
        slot = self.final.at[self.at.dp_at(-e)]
        return send(slot, slot, self.all_sem, (e,), self.at.on_dp(self.at.dp_at(e)))

    def start(self, lhs_ref, rhs_ref):
        for first in range(0, self.cols, CHUNK):
            out = self.product(lhs_ref, rhs_ref, 1 - self.at.core, first)
            self.pair_out[:, :, first:first + CHUNK] = out.astype(BF16)
        self.pair_copy().start()

    def over_dp(self, lhs_ref, rhs_ref):
        sz = self.sz
        self.pair_copy().wait_recv()
        part_cols = self.cols // sz.col_parts
        for first in range(0, self.cols, CHUNK):
            out = self.product(lhs_ref, rhs_ref, self.at.core, first)
            out = (out + self.pair_in[:, :, first:first + CHUNK].astype(F32)).astype(BF16)
            col = first // part_cols
            inner = first - col * part_cols
            for row in range(sz.row_parts):
                self.dp_out[row * sz.col_parts + col, :, :, inner:inner + CHUNK] = out[
                    :, row * sz.part_rows:(row + 1) * sz.part_rows, :
                ]
        for e in range(1, sz.n_dp):
            self.dp_copy(e).start()

    def over_chips(self):
        sz = self.sz
        total = self.dp_out[self.at.dp].astype(F32)
        for e in range(1, sz.n_dp):
            self.dp_copy(e).wait_recv()
            total = total + self.dp_in[e - 1].astype(F32)
        self.z_out[...] = total.astype(BF16)
        for d in range(1, sz.chips):
            self.z_copy(d).start()

    def to_all(self):
        sz = self.sz
        total = self.z_out[self.at.chip].astype(F32)
        for d in range(1, sz.chips):
            self.z_copy(d).wait_recv()
            total = total + self.z_in[d - 1].astype(F32)
        self.final[self.at.dp] = total.astype(BF16)
        for e in range(1, sz.n_dp):
            self.all_copy(e).start()

    def finish(self, outs):
        sz = self.sz
        for e in range(1, sz.n_dp):
            self.all_arrival(e).wait_recv()
        part_cols = self.cols // sz.col_parts
        out_cols = outs[0].shape[1]
        for part in range(sz.n_dp):
            row, col = part // sz.col_parts, part % sz.col_parts
            for first in range(0, part_cols, CHUNK):
                at = col * part_cols + first
                outs[at // out_cols][
                    row * sz.part_rows:(row + 1) * sz.part_rows,
                    at % out_cols:at % out_cols + CHUNK,
                ] = self.final[part, :, first:first + CHUNK].astype(F32)
        self.pair_copy().wait_send()
        for e in range(1, sz.n_dp):
            self.dp_copy(e).wait_send()
            self.all_copy(e).wait_send()
        for d in range(1, sz.chips):
            self.z_copy(d).wait_send()


def kernel(
    sz, plen_ref, bound_ref, x_ref, up_ref, gain_ref, wq_ref, wk_ref, wv_ref, wo_ref,
    din_ref, gq_ref, gk_ref, gv_ref, go_ref, gg_ref,
    hidden, hidden_t, q_t, q_s, da_t, da_s, kv, expo, tops, sums, attn_t, delta, acc, dq, dkv,
    dhid, dkv_out, dkv_in, dkz_out, dkz_in, gain_in, gain_all,
    kv_sem, fwd_sem, dpair_sem, dz_sem, gain_sem, gain_all_sem, *item_refs,
):
    at = Place(sz)
    tok, heads, chips, lanes = sz.tok, sz.heads, sz.chips, sz.lanes
    per = len(item_refs) // 3
    hq = heads * HS
    item_out = Item(at, up_ref.shape[1], item_refs[:per])
    item_q = Item(at, hq, item_refs[per:2 * per])
    item_kv = Item(at, 2 * HS, item_refs[2 * per:])
    scaling = HS ** (-0.5)
    seq = tok * sz.n_blk

    barrier = pltpu.get_barrier_semaphore()
    for b in range(1, sz.n_blk):
        peer = (at.dp, lax.rem(at.blk + b, sz.n_blk))
        pl.semaphore_signal(barrier, inc=1, device_id=peer, device_id_type=MESH)
    for e in range(1, sz.n_dp):
        pl.semaphore_signal(barrier, inc=1, device_id=at.on_dp(at.dp_at(e)), device_id_type=MESH)

    def normed_inv():
        xf = x_ref[...].astype(F32)
        inv = lax.rsqrt(jnp.mean(xf * xf, axis=-1, keepdims=True) + EPS)
        return xf * inv, inv

    normed, _ = normed_inv()
    hidden[...] = (normed * gain_ref[...]).astype(BF16)
    kv[at.blk, :, :HS] = dot_nn(hidden[...], wk_ref[...]).astype(BF16)
    kv[at.blk, :, HS:] = dot_nn(hidden[...], wv_ref[...]).astype(BF16)
    pl.semaphore_wait(barrier, sz.n_blk - 1 + sz.n_dp - 1)

    def kv_copy(d):
        mine = kv.at[at.blk]
        return send(mine, mine, kv_sem, (d,), at.on_chip(at.chip_at(d)))

    def kv_arrival(d):
        slot = kv.at[2 * at.chip_at(-d) + at.core]
        return send(slot, slot, kv_sem, (d,), at.on_chip(at.chip_at(d)))

    def kv_forward(d):
        slot = kv.at[2 * at.chip_at(-d) + at.core]
        return send(slot, slot, fwd_sem, (d,), at.sibling())

    def kv_forwarded(d):
        slot = kv.at[2 * at.chip_at(-d) + 1 - at.core]
        return send(slot, slot, fwd_sem, (d,), at.sibling())

    for d in range(1, chips):
        kv_copy(d).start()
    kv_forward(0).start()

    for h in range(heads):
        cols = slice(h * HS, (h + 1) * HS)
        toks = slice(h * tok, (h + 1) * tok)
        one = dot_nn(hidden[...], wq_ref[:, cols])
        q_s[toks, :] = one.astype(BF16)
        q_t[:, toks] = one.T.astype(BF16)
        one = dot_nt(up_ref[...], wo_ref[cols, :])
        da_s[toks, :] = one.astype(BF16)
        da_t[:, toks] = one.T.astype(BF16)
    for b in range(sz.n_blk):
        piece = hidden[:, b * sz.rows:(b + 1) * sz.rows].astype(F32)
        hidden_t[b] = piece.T.astype(BF16)

    plen = plen_ref[0]
    edge = bound_ref[0] * BLOCK
    q_pos = at.blk * tok + lax.rem(lax.broadcasted_iota(jnp.int32, (1, lanes), 1), tok)

    def score_block(b):
        k_pos = b * tok + lax.broadcasted_iota(jnp.int32, (tok, 1), 0)
        key_ok = (k_pos < plen) | (k_pos >= seq - ACT)
        first_seen = jnp.where(key_ok, jnp.where(k_pos < edge, -1, k_pos), seq)
        for h in range(heads):
            toks = slice(h * tok, (h + 1) * tok)
            scores = dot_nn(kv[b, :, :HS], q_t[:, toks]) * scaling
            scores = jnp.where(q_pos[:, toks] >= first_seen, scores, NEG)
            top = jnp.max(scores, axis=0, keepdims=True)
            values = jnp.exp(scores - top)
            expo[b, :, toks] = values
            tops[b, :, toks] = top
            sums[b, :, toks] = jnp.sum(values, axis=0, keepdims=True)

    score_block(at.blk)

    def arrive(d, carry):
        kv_arrival(d).wait_recv()
        kv_forward(d).start()
        score_block(2 * at.chip_at(-d) + at.core)
        kv_forwarded(d - 1).wait_recv()
        score_block(2 * at.chip_at(1 - d) + 1 - at.core)
        return carry

    lax.fori_loop(1, chips, arrive, 0)
    kv_forwarded(chips - 1).wait_recv()
    score_block(2 * at.chip_at(1 - chips) + 1 - at.core)

    top = jnp.max(tops[...], axis=0)
    scale_all = jnp.exp(tops[...] - top[None])
    total = jnp.sum(scale_all * sums[...], axis=0)
    tops[...] = scale_all / total[None]

    acc[...] = jnp.zeros_like(acc)

    def attn_step(b, carry):
        for h in range(heads):
            toks = slice(h * tok, (h + 1) * tok)
            probs = expo[b, :, toks] * tops[b, :, toks]
            expo[b, :, toks] = probs
            acc[:, toks] += dot_tn(kv[b, :, HS:], probs.astype(BF16))
        return carry

    lax.fori_loop(0, sz.n_blk, attn_step, 0)

    per_head = HS // sz.rows
    for h in range(heads):
        toks = slice(h * tok, (h + 1) * tok)
        one = acc[:, toks].astype(BF16)
        delta[:, toks] = jnp.sum(da_t[:, toks].astype(F32) * one.astype(F32), axis=0, keepdims=True)
        for j in range(per_head):
            attn_t[h * per_head + j] = one[j * sz.rows:(j + 1) * sz.rows, :]

    item_out.start(attn_t, up_ref)

    acc[...] = jnp.zeros_like(acc)

    def grads_block(b):
        dk = jnp.zeros((tok, HS), F32)
        dv = jnp.zeros((tok, HS), F32)
        for h in range(heads):
            toks = slice(h * tok, (h + 1) * tok)
            probs = expo[b, :, toks]
            dprobs = dot_nn(kv[b, :, HS:], da_t[:, toks])
            dscores = (probs * (dprobs - delta[:, toks])).astype(BF16)
            acc[:, toks] += dot_tn(kv[b, :, :HS], dscores)
            dk = dk + dot_nn(dscores, q_s[toks, :])
            dv = dv + dot_nn(probs.astype(BF16), da_s[toks, :])
        return dk * scaling, dv

    def dpair_copy(d):
        chip = at.chip_at(d)
        return send(dkv_out.at[chip], dkv_in.at[chip], dpair_sem, (d,), at.sibling())

    def dz_copy(d):
        chip = at.chip_at(d)
        return send(dkz_out.at[d - 1], dkz_in.at[d - 1], dz_sem, (d,), at.on_chip(chip))

    def pair_sum(d):
        chip = at.chip_at(d)
        dk, dv = grads_block(2 * chip + 1 - at.core)
        dkv_out[chip, :, :HS] = dk.astype(BF16)
        dkv_out[chip, :, HS:] = dv.astype(BF16)
        dpair_copy(d).start()
        dk, dv = grads_block(2 * chip + at.core)
        dpair_copy(d).wait_recv()
        dk = dk + dkv_in[chip, :, :HS].astype(F32)
        dv = dv + dkv_in[chip, :, HS:].astype(F32)
        return dk, dv

    def grads_step(d, carry):
        dk, dv = pair_sum(d)
        dkz_out[d - 1, :, :HS] = dk.astype(BF16)
        dkz_out[d - 1, :, HS:] = dv.astype(BF16)
        dz_copy(d).start()
        return carry

    lax.fori_loop(1, chips, grads_step, 0)
    dk, dv = pair_sum(0)
    dhid[:, :HS] = dk
    dhid[:, HS:2 * HS] = dv

    item_out.over_dp(attn_t, up_ref)
    for h in range(heads):
        toks = slice(h * tok, (h + 1) * tok)
        dq[:, h * HS:(h + 1) * HS] = (acc[:, toks] * scaling).T.astype(BF16)
    item_q.start(hidden_t, dq)
    item_q.over_dp(hidden_t, dq)

    dk = dhid[:, :HS]
    dv = dhid[:, HS:2 * HS]
    for d in range(1, chips):
        dz_copy(d).wait_recv()
        dk = dk + dkz_in[d - 1, :, :HS].astype(F32)
        dv = dv + dkz_in[d - 1, :, HS:].astype(F32)
    dkv[:, :HS] = dk.astype(BF16)
    dkv[:, HS:] = dv.astype(BF16)
    item_kv.start(hidden_t, dkv)
    item_out.over_chips()
    for first in range(0, sz.width, CHUNK):
        cols = slice(first, first + CHUNK)
        dhid[:, cols] = (
            dot_nt(dq[...], wq_ref[cols, :])
            + dot_nt(dkv[:, :HS], wk_ref[cols, :])
            + dot_nt(dkv[:, HS:], wv_ref[cols, :])
        )
    item_kv.over_dp(hidden_t, dkv)

    def gain_copy(b):
        peer = (at.dp, lax.rem(at.blk + b, sz.n_blk))
        return send(gain_in.at[0], gain_in.at[b], gain_sem, (b,), peer)

    def gain_share(e):
        mine = gain_all.at[at.dp]
        return send(mine, mine, gain_all_sem, (e,), at.on_dp(at.dp_at(e)))

    def gain_arrival(e):
        slot = gain_all.at[at.dp_at(-e)]
        return send(slot, slot, gain_all_sem, (e,), at.on_dp(at.dp_at(e)))

    normed, inv = normed_inv()
    gain_in[0] = jnp.sum(dhid[...] * normed, axis=0, keepdims=True)
    for b in range(1, sz.n_blk):
        gain_copy(b).start()
    item_q.over_chips()
    item_out.to_all()

    normed, inv = normed_inv()
    scaled = dhid[...] * gain_ref[...]
    middle = jnp.mean(scaled * normed, axis=-1, keepdims=True)
    din_ref[...] = (up_ref[...].astype(F32) + inv * (scaled - normed * middle)).astype(BF16)

    total = gain_in[0]
    for b in range(1, sz.n_blk):
        gain_copy(b).wait_recv()
        total = total + gain_in[b]
    gain_all[at.dp] = total
    for e in range(1, sz.n_dp):
        gain_share(e).start()
    item_kv.over_chips()
    item_q.to_all()
    item_kv.to_all()
    item_out.finish((go_ref,))
    for e in range(1, sz.n_dp):
        gain_arrival(e).wait_recv()
    total = gain_all[0]
    for e in range(1, sz.n_dp):
        total = total + gain_all[e]
    for b in range(sz.n_blk):
        @pl.when(at.blk == b)
        def _():
            gg_ref[...] = total[:, b * sz.rows:(b + 1) * sz.rows]
    item_q.finish((gq_ref,))
    item_kv.finish((gk_ref, gv_ref))

    for d in range(1, chips):
        kv_copy(d).wait_send()
        dz_copy(d).wait_send()
    for d in range(chips):
        kv_forward(d).wait_send()
        dpair_copy(d).wait_send()
    for b in range(1, sz.n_blk):
        gain_copy(b).wait_send()
    for e in range(1, sz.n_dp):
        gain_share(e).wait_send()


def per_device(n_dp, n_blk, inputs, upstream, gain, w_query, w_key, w_value, w_out, prefix_len, bound):
    tok, width = inputs.shape[1:]
    hq = w_query.shape[1]
    sz = Sizes(n_dp, n_blk, tok, width, hq)
    chips = sz.chips
    vm, dma = pltpu.VMEM, pltpu.SemaphoreType.DMA
    scratch = [
        vm((tok, width), BF16),
        vm((n_blk, sz.rows, tok), BF16),
        vm((HS, sz.lanes), BF16),
        vm((sz.lanes, HS), BF16),
        vm((HS, sz.lanes), BF16),
        vm((sz.lanes, HS), BF16),
        vm((n_blk, tok, 2 * HS), BF16),
        vm((n_blk, tok, sz.lanes), F32),
        vm((n_blk, 1, sz.lanes), F32),
        vm((n_blk, 1, sz.lanes), F32),
        vm((n_blk, sz.rows, tok), BF16),
        vm((1, sz.lanes), F32),
        vm((HS, sz.lanes), F32),
        vm((tok, hq), BF16),
        vm((tok, 2 * HS), BF16),
        vm((tok, width), F32),
        vm((chips, tok, 2 * HS), BF16),
        vm((chips, tok, 2 * HS), BF16),
        vm((chips - 1, tok, 2 * HS), BF16),
        vm((chips - 1, tok, 2 * HS), BF16),
        vm((n_blk, 1, width), F32),
        vm((n_dp, 1, width), F32),
        dma((2, chips)),
        dma((2, chips)),
        dma((2, chips)),
        dma((2, chips)),
        dma((2, n_blk)),
        dma((2, n_dp)),
        *sz.item_scratch(width),
        *sz.item_scratch(hq),
        *sz.item_scratch(2 * HS),
    ]
    smem = pl.BlockSpec(memory_space=pltpu.SMEM)
    vmem = pl.BlockSpec(memory_space=pltpu.VMEM)
    shape = jax.ShapeDtypeStruct
    d_in, g_query, g_key, g_value, g_out, g_gain = pl.pallas_call(
        functools.partial(kernel, sz),
        out_shape=(
            shape((tok, width), BF16),
            shape((sz.rows, hq), F32),
            shape((sz.rows, HS), F32),
            shape((sz.rows, HS), F32),
            shape((sz.rows, width), F32),
            shape((1, sz.rows), F32),
        ),
        in_specs=[smem, smem] + [vmem] * 7,
        out_specs=(vmem,) * 6,
        scratch_shapes=scratch,
        compiler_params=pltpu.CompilerParams(
            collective_id=0, has_side_effects=True, vmem_limit_bytes=60 * 1024 * 1024
        ),
    )(prefix_len, bound, inputs[0], upstream[0], gain[None], w_query, w_key, w_value, w_out)
    return d_in[None], g_query, g_key, g_value, g_out, g_gain[0]


def solution(mesh):
    placed = (P("dp", "blk", None), P("dp", "blk", None), P(), P(), P(), P(), P(), P("dp"), P("dp"))
    return jax.shard_map(
        functools.partial(per_device, mesh.shape["dp"], mesh.shape["blk"]),
        mesh=mesh,
        in_specs=placed,
        out_specs=(
            P("dp", "blk", None),
            P("blk", None),
            P("blk", None),
            P("blk", None),
            P("blk", None),
            P("blk"),
        ),
        check_vma=False,
    )
```

time: 353 us -> 99.1 us (0.28)
  waiting for transfers between devices: 178 us -> 0 us
  Pallas kernels: 0 us -> 90.4 us
  matrix products: 84 us -> 0 us
  other arithmetic: 34.1 us -> 0 us
  blocking collectives: 23.8 us -> 0 us
  between operations: 16.3 us -> 1.97 us
  local copies, waits for them, and re-layouts: 15.2 us -> 6.45 us
    reduce_scatter x5 -> x0, waiting for transfers between devices: 139 us -> none  [the longest x1 36.5 us: per_device(): lax.psum_scatter(g_out.astype(jnp.bfloat16), 'blk', scatter_dimension=0,...]
    pallas_call x0 -> x1, Pallas kernels: none -> 90.4 us  [per_device(): pl.pallas_call(functools.partial(kernel, sz), out_shape=(shape((tok, widt...]
    dot_general x30 -> x0, matrix products: 84 us -> none  [the longest x9 21.5 us: scores_of(): jnp.einsum('thd,kd->htk', q_three, key_rows, preferred_element_type=jnp.f...]
    psum x1 -> x0, waiting for transfers between devices: 19.3 us -> none  [per_device(): lax.psum(shares[0].astype(jnp.bfloat16), 'dp').astype(jnp.float32)]
    all_gather x2 -> x0, waiting for transfers between devices: 19 us -> none  [the longest x1 11.4 us: per_device(): lax.all_gather(values, 'blk', axis=0, tiled=True)]
    unnamed x1 -> x0, blocking collectives: 13.7 us -> none
    psum x1 -> x0, blocking collectives: 10.1 us -> none  [per_device(): lax.psum(shares[4].astype(jnp.bfloat16), 'dp').astype(jnp.float32)]
    convert_element_type x6 -> x0, other arithmetic: 8.43 us -> none  [the longest x1 1.79 us: per_device(): lax.psum(shares[0].astype(jnp.bfloat16), 'dp').astype(jnp.float32)]
  transfers between devices with their start and end apart: 8 -> 0, of which waited for: 8 -> 0; matrix products, arithmetic and copies ran while one was open for 22% -> 0% of each run, Pallas kernels for 0% -> 0%
where the time goes in v1:
time: 99.1 us; the launch traced here: 98.9 us
  Pallas kernels  90.4 us (91%)
  local copies, waits for them, and re-layouts  6.45 us (7%)
  between operations  1.97 us (2%)
    pallas_call x1, Pallas kernels, per_device(): pl.pallas_call(functools.partial(kernel, sz), out_shape=(shape((tok, widt...  90.4 us
    unnamed x14, local copies, waits for them, and re-layouts  6.45 us

profile of v1, /device:TPU:0, one launch (start us, length us, event | category | flops | bytes accessed | tf_op | source)
XLA Modules:
  0.0 98.9 jit_solution(5464878425695036265)
XLA Ops:
  1.9 90.4 %shard_map.136 = (bf16[256,1024]{1,0:T(8,128)(2,1)}, f32[128,1024]{1,0:T(8,128)}, f32[128,256]{1,0:T(8,128)}, f32[128,256]{1,0:T(8,128)}, f32[128,1024]{1,0:T(8,128)}, /*index=5*/f32[1,128]{1,0:T(1,128)}) custom-call(s32[1]{0:T(128)S(6)} %copy.21.plen_ref, s32[1]{0:T(128)S(6)} %copy.22.bound_ref, bf16[256,1024]{1,0:T(8,128)(2,1)} %bitcast.5, ...), custom_call_target="tpu_custom_call" | custom-call | tf_op jit(solution)/shard_map/pallas_call | solution.py:495
  92.4 0.0 copy-start.2
  92.4 0.0 copy-start.1
  92.4 0.0 copy-start
  92.4 0.0 copy-start.3
  92.4 1.9 %copy.23 = bf16[1,256,1024]{2,1,0:T(8,128)(2,1)} copy(bf16[1,256,1024]{2,1,0:T(8,128)(2,1)} %bitcast.7) | data formatting | bytes 1048576
  94.3 1.9 %copy.24 = f32[128,1024]{1,0:T(8,128)} copy(f32[128,1024]{1,0:T(8,128)} %get-tuple-element.25) | data formatting | bytes 1048576
  96.2 0.0 copy-done.2
  96.2 0.7 copy.25
  96.9 0.0 copy-done.1
  96.9 0.7 copy.26
  97.5 0.0 copy-done
  97.6 0.8 copy.27
  98.3 0.0 copy-done.3
  98.3 0.5 copy.28
Async XLA Ops:
  92.4 3.9 %copy-start.2 = (f32[128,256]{1,0:T(8,128)S(1)}, f32[128,256]{1,0:T(8,128)}, u32[]{:S(2)}) copy-start(f32[128,256]{1,0:T(8,128)} %get-tuple-element.26) | copy-start | bytes 393220
  92.4 4.5 %copy-start.1 = (f32[128,256]{1,0:T(8,128)S(1)}, f32[128,256]{1,0:T(8,128)}, u32[]{:S(2)}) copy-start(f32[128,256]{1,0:T(8,128)} %get-tuple-element.27) | copy-start | bytes 393220
  92.4 5.2 %copy-start = (f32[128,1024]{1,0:T(8,128)S(1)}, f32[128,1024]{1,0:T(8,128)}, u32[]{:S(2)}) copy-start(f32[128,1024]{1,0:T(8,128)} %get-tuple-element.28) | copy-start | bytes 1572868
  92.4 5.9 %copy-start.3 = (f32[1,128]{1,0:T(1,128)S(1)}, f32[1,128]{1,0:T(1,128)}, u32[]{:S(2)}) copy-start(f32[1,128]{1,0:T(1,128)} %get-tuple-element.17) | copy-start | bytes 1540
